TPU v7x, 256 devices: a whole 4x4x8 slice. The times are simulated.
256 devices in a mesh: state: 32 (over z, x_hi, core), seq: 8 (over y, x_lo).
Axes of the slice: x: 4 (x_hi: 2, x_lo: 2; x = x_hi * 2 + x_lo), y: 4, z: 8, core: 2. Of those that a mesh axis runs over, the one named last changes fastest.
Arguments:
- feature_u: bfloat16 [65536, 4096], P('state', 'seq'), may hold values from 0.0001 to 25000, as said below
- feature_v: bfloat16 [65536, 4096], P('state', 'seq'), may hold values from 0.0001 to 25000, as said below
- emission: bfloat16 [10240, 65536], P('seq', 'state'), may hold values from 0.099609375 to 10
- word_ids: int32 [64, 4], replicated, may hold values from 0 to 10239
- scales: float32 [64, 4], P('seq'), may hold values from 1 to 4
- backward_end: float32 [64, 65536], P('seq', 'state'), may hold values from 0.25 to 4
Outputs:
- backward_messages: float32 [4, 64, 65536], P(None, 'seq', 'state')
Inputs may be any that keep to these rules, and one draw needn't show every extreme that they name: `feature_u`: positive transition features. `feature_v`: positive transition features.
All inputs are finite; a program needn't handle non-finite values.
Results may differ from a plain program's by a relative error of at most 0.0022.
Values may be sent and summed in bfloat16 or wider, within the bound.
A program may use at most 64 MiB of HBM per device.

v0:
```python
import jax
import jax.numpy as jnp
from jax import lax
from jax.sharding import PartitionSpec as P


def rank_message(partial_sum):
    return lax.psum(partial_sum, "state").astype(jnp.bfloat16)


def project(message, feature_u):
    return lax.dot_general(
        message, feature_u, (((1,), (1,)), ((), ())), preferred_element_type=jnp.float32
    )


def body(feature_u, feature_v, emission, word_ids, scales, backward_end):
    table_rows = emission.shape[0]
    local_ids = word_ids - lax.axis_index("seq") * table_rows
    inside = (local_ids >= 0) & (local_ids < table_rows)
    gathered = jnp.take(emission, jnp.clip(local_ids, 0, table_rows - 1), axis=0)
    selected = jnp.where(inside[:, :, None], gathered.astype(jnp.float32), 0.0)
    picked = lax.psum_scatter(selected.astype(jnp.bfloat16), "seq", scatter_dimension=0, tiled=True)
    column_mass = lax.psum(jnp.sum(feature_v, axis=0, dtype=jnp.float32), "state")
    norm_part = jnp.dot(feature_u.astype(jnp.float32), column_mass, precision=lax.Precision.HIGHEST)
    row_norm = lax.psum(norm_part, "seq")
    steps_count = picked.shape[1]
    seq_rows = picked.shape[0]
    results = [None] * steps_count
    current = backward_end
    for position in reversed(range(steps_count)):
        weighted = (picked[:, position, :].astype(jnp.float32) * current).astype(jnp.bfloat16)
        partial_sum = jnp.dot(
            lax.all_gather(weighted, "seq", axis=0, tiled=True),
            feature_v,
            preferred_element_type=jnp.float32,
        )
        message = rank_message(partial_sum)

        def expand(first, how_many, message=message):
            return project(message, feature_u)

        unscaled = lax.psum_scatter(
            expand(jnp.int32(0), lax.axis_size("seq") * seq_rows),
            "seq",
            scatter_dimension=0,
            tiled=True,
        )
        current = unscaled / (row_norm[None, :] * scales[:, position : position + 1])
        results[position] = current
    return jnp.stack(results)


def solution(mesh):
    placed = (
        P("state", "seq"),
        P("state", "seq"),
        P("seq", "state"),
        P(),
        P("seq", None),
        P("seq", "state"),
    )
    return jax.shard_map(
        body, mesh=mesh, in_specs=placed, out_specs=P(None, "seq", "state"), check_vma=False
    )
```

profile of v0, /device:TPU:4, one launch (start us, length us, event | category | flops | bytes accessed | tf_op | source)
XLA Modules:
  0.0 871.8 jit_solution(15606571699578114388)
XLA Ops:
  7.6 5.5 gather_fusion
  14.6 1.9 select_convert_fusion
  16.5 1.6 copy.15
  18.2 1.9 convert_reduce_fusion
  20.1 44.5 %reduce-scatter.16.cloned.1.call-done = bf16[8,8192]{1,0:T(8,128)(2,1)} async-done(((bf16[64,8192]{1,0:T(8,128)(2,1)}), bf16[8,8192]{1,0:T(8,128)(2,1)}) %reduce-scatter.16.cloned.1.call-update) | async-done | bytes 131088
  65.4 28.7 %all_gather.12 = bf16[64,2048]{1,0:T(8,128)(2,1)S(1)} all-gather(bf16[8,2048]{1,0:T(8,128)(2,1)S(1)} %fusion), channel_id=1, replica_groups=mesh['state'=32,'seq'=8] {'seq'}, dimensions={0}, use_global_device_ids=true | all-gather | bytes 294912 | tf_op jit(solution)/shard_map/all_gather | solution.py:34
  94.1 2.1 fusion.15
  96.2 125.1 %all-reduce.5 = (bf16[64,512]{1,0:T(8,128)(2,1)S(1)}, f32[512]{0:T(512)S(1)}) all-reduce(f32[64,512]{1,0:T(8,128)S(1)} %fusion.15, f32[512]{0:T(512)S(1)} %convert_reduce_fusion), channel_id=1, replica_groups=mesh['state'=32,'seq'=8] {'state'}, use_global_device_ids=true, to_apply=%region_1.2 | all-reduce | flops 33280 | bytes 200704 | tf_op jit(solution)/shard_map/psum | solution.py:8
  221.3 1.5 fusion.23
  222.9 1.7 fusion.16
  224.6 18.0 %psum.44 = f32[2048]{0:T(1024)S(1)} all-reduce(f32[2048]{0:T(1024)S(1)} %bitcast.66), channel_id=1, replica_groups=mesh['state'=32,'seq'=8] {'seq'}, use_global_device_ids=true, to_apply=%region_5.6 | all-reduce | flops 2048 | bytes 16384 | tf_op jit(solution)/shard_map/psum | solution.py:26
  242.7 22.7 %reduce-scatter.8.cloned.1.call-done = f32[8,2048]{1,0:T(8,128)} async-done(((f32[64,2048]{1,0:T(8,128)}), f32[8,2048]{1,0:T(8,128)}) %reduce-scatter.8.cloned.1.call-update) | async-done | bytes 65552 | tf_op jit(solution)/shard_map/reduce_scatter | solution.py:43
  266.3 28.7 %all_gather.13 = bf16[64,2048]{1,0:T(8,128)(2,1)S(1)} all-gather(bf16[8,2048]{1,0:T(8,128)(2,1)S(1)} %get-tuple-element.13), channel_id=1, replica_groups=mesh['state'=32,'seq'=8] {'seq'}, dimensions={0}, use_global_device_ids=true | all-gather | bytes 294912 | tf_op jit(solution)/shard_map/all_gather | solution.py:34
  295.0 2.1 fusion.17
  297.1 123.8 %all-reduce.6 = bf16[64,512]{1,0:T(8,128)(2,1)S(1)} all-reduce(f32[64,512]{1,0:T(8,128)S(1)} %fusion.17), channel_id=1, replica_groups=mesh['state'=32,'seq'=8] {'state'}, use_global_device_ids=true, to_apply=%region_6.7 | all-reduce | flops 32768 | bytes 196608 | tf_op jit(solution)/shard_map/psum | solution.py:8
  422.5 42.2 %reduce-scatter.10.cloned.1.call-done = f32[8,2048]{1,0:T(8,128)} async-done(((f32[64,2048]{1,0:T(8,128)}), f32[8,2048]{1,0:T(8,128)}) %reduce-scatter.10.cloned.1.call-update) | async-done | bytes 65552 | tf_op jit(solution)/shard_map/reduce_scatter | solution.py:43
  465.7 28.8 %all_gather.14 = bf16[64,2048]{1,0:T(8,128)(2,1)S(1)} all-gather(bf16[8,2048]{1,0:T(8,128)(2,1)S(1)} %get-tuple-element.11), channel_id=1, replica_groups=mesh['state'=32,'seq'=8] {'seq'}, dimensions={0}, use_global_device_ids=true | all-gather | bytes 294912 | tf_op jit(solution)/shard_map/all_gather | solution.py:34
  494.5 2.1 fusion.18
  496.6 123.7 %all-reduce.7 = bf16[64,512]{1,0:T(8,128)(2,1)S(1)} all-reduce(f32[64,512]{1,0:T(8,128)S(1)} %fusion.18), channel_id=1, replica_groups=mesh['state'=32,'seq'=8] {'state'}, use_global_device_ids=true, to_apply=%region_8.9 | all-reduce | flops 32768 | bytes 196608 | tf_op jit(solution)/shard_map/psum | solution.py:8
  621.9 42.5 %reduce-scatter.12.cloned.1.call-done = f32[8,2048]{1,0:T(8,128)} async-done(((f32[64,2048]{1,0:T(8,128)}), f32[8,2048]{1,0:T(8,128)}) %reduce-scatter.12.cloned.1.call-update) | async-done | bytes 65552 | tf_op jit(solution)/shard_map/reduce_scatter | solution.py:43
  665.3 28.7 %all_gather.15 = bf16[64,2048]{1,0:T(8,128)(2,1)S(1)} all-gather(bf16[8,2048]{1,0:T(8,128)(2,1)S(1)} %get-tuple-element.9), channel_id=1, replica_groups=mesh['state'=32,'seq'=8] {'seq'}, dimensions={0}, use_global_device_ids=true | all-gather | bytes 294912 | tf_op jit(solution)/shard_map/all_gather | solution.py:34
  694.1 2.1 fusion.19
  696.1 123.7 %all-reduce.8 = bf16[64,512]{1,0:T(8,128)(2,1)S(1)} all-reduce(f32[64,512]{1,0:T(8,128)S(1)} %fusion.19), channel_id=1, replica_groups=mesh['state'=32,'seq'=8] {'state'}, use_global_device_ids=true, to_apply=%region_10.11 | all-reduce | flops 32768 | bytes 196608 | tf_op jit(solution)/shard_map/psum | solution.py:8
  821.4 42.2 %reduce-scatter.14.cloned.1.call-done = f32[8,2048]{1,0:T(8,128)} async-done(((f32[64,2048]{1,0:T(8,128)}), f32[8,2048]{1,0:T(8,128)}) %reduce-scatter.14.cloned.1.call-update) | async-done | bytes 65552 | tf_op jit(solution)/shard_map/reduce_scatter | solution.py:43
  (35 shorter events, 12.6 us)
Async XLA Ops:
  6.5 214.7 %copy-start = (bf16[2048,512]{1,0:T(8,128)(2,1)S(1)}, bf16[2048,512]{1,0:T(8,128)(2,1)}, u32[]{:S(2)}) copy-start(bf16[2048,512]{1,0:T(8,128)(2,1)} %param.6) | copy-start | bytes 6291460
  6.5 58.1 %reduce-scatter.16.cloned.1.call-start = ((), (), s32[]{:S(2)}) async-start(), calls=%async_computation.9 | async-start | bytes 1179648
  18.1 46.5 %copy-start.2 = (f32[8,2048]{1,0:T(8,128)S(1)}, f32[8,2048]{1,0:T(8,128)}, u32[]{:S(2)}) copy-start(f32[8,2048]{1,0:T(8,128)} %param.11) | copy-start | bytes 196612
  18.1 247.2 %reduce-scatter.8.cloned.1.call-start = ((), (), s32[]{:S(2)}) async-start(), calls=%async_computation.5 | async-start | bytes 589824 | tf_op jit(solution)/shard_map/reduce_scatter | solution.py:43
  96.2 126.7 %copy-start.3 = (f32[8,4]{0,1:T(4,128)S(1)}, f32[8,4]{0,1:T(4,128)}, u32[]{:S(2)}) copy-start(f32[8,4]{0,1:T(4,128)} %param.10) | copy-start | bytes 388
  221.3 44.1 %copy-start.1 = (bf16[8,8192]{1,0:T(8,128)(2,1)S(1)}, bf16[8,8192]{1,0:T(8,128)(2,1)}, u32[]{:S(2)}) copy-start(bf16[8,8192]{1,0:T(8,128)(2,1)} %reduce-scatter.16.cloned.1.call-done) | copy-start | bytes 393220
  222.8 241.9 %reduce-scatter.10.cloned.1.call-start = ((), (), s32[]{:S(2)}) async-start(), calls=%async_computation.6 | async-start | bytes 589824 | tf_op jit(solution)/shard_map/reduce_scatter | solution.py:43
  422.4 241.9 %reduce-scatter.12.cloned.1.call-start = ((), (), s32[]{:S(2)}) async-start(), calls=%async_computation.7 | async-start | bytes 589824 | tf_op jit(solution)/shard_map/reduce_scatter | solution.py:43
  621.8 241.8 %reduce-scatter.14.cloned.1.call-start = ((), (), s32[]{:S(2)}) async-start(), calls=%async_computation.8 | async-start | bytes 589824 | tf_op jit(solution)/shard_map/reduce_scatter | solution.py:43
Sparse Core Ops, SparseCore 0:
  18.3 46.3 reduce-scatter.15
  223.0 42.3 reduce-scatter.7
  422.6 42.1 reduce-scatter.9
  621.9 42.4 reduce-scatter.11
  821.5 42.0 reduce-scatter.13
where the time goes:
time: 873 us; the launch traced here: 872 us
  blocking collectives  629 us (72%)
  waiting for transfers between devices  194 us (22%)
  matrix products  16.1 us (2%)
  between operations  13.2 us (2%)
  other arithmetic  9.88 us (1%)
  local copies, waits for them, and re-layouts  8.81 us (1%)
    psum x4, blocking collectives, rank_message(): return lax.psum(partial_sum, 'state').astype(jnp.bfloat16)  496 us
    reduce_scatter x4, waiting for transfers between devices, body(): lax.psum_scatter(expand(jnp.int32(0), lax.axis_size('seq') * seq_rows), '...  150 us
    all_gather x4, blocking collectives, body(): lax.all_gather(weighted, 'seq', axis=0, tiled=True)  115 us
    unnamed x6, waiting for transfers between devices  44.6 us
    psum x1, blocking collectives, body(): row_norm = lax.psum(norm_part, 'seq')  18 us
  transfers between devices with their start and end apart: 5, of which 5 were waited for; matrix products, arithmetic and copies ran while one was open for 0% of the time, Pallas kernels for 0%

commit v1 on v0

v1 whole, which is shorter than its diff:
```python
import jax
import jax.numpy as jnp
from jax import lax
from jax.experimental import pallas as pl
from jax.experimental.pallas import tpu as pltpu
from jax.sharding import PartitionSpec as P

CHAINS = 1
STATES = 2048
RANK = 512
SEQS = 64
STEPS = 4
N_SEQ = 8
N_STATE = 32
BLOCK = STATES // N_SEQ
TILES = 16
ROWS = SEQS // CHAINS
HALF = TILES // CHAINS
BF = jnp.bfloat16
F32 = jnp.float32


def kernel(
    u_hbm, v_hbm, em_hbm, ids_hbm, sc_hbm, be_hbm, out_hbm,
    u, v, em, ids, sc, be,
    scs, ends, csbuf, nsend, nrecv,
    emsend, emrecv, wbuf, part, arr, red, msg, rsend, rrecv, rown, bk,
    load_sem, init_send, init_recv, sc_recv, cs_send, cs_recv, n_send, n_recv,
    em_send, em_recv, ag_send, ag_recv, ar_send, ar_recv, red_send, msg_recv,
    rs_send, rs_recv, out_send, out_recv, out_local,
):
    my_state = lax.axis_index("state")
    my_seq = lax.axis_index("seq")

    def peer(d):
        return lax.rem(my_seq + d, N_SEQ)

    def remote(src, dst, send, recv, state, seq):
        return pltpu.make_async_remote_copy(
            src_ref=src, dst_ref=dst, send_sem=send, recv_sem=recv,
            device_id={"state": state, "seq": seq},
            device_id_type=pl.DeviceIdType.MESH,
        )

    def wait(ref, sem):
        pltpu.make_async_copy(ref, ref, sem).wait()

    loads = [
        pltpu.make_async_copy(src, dst, load_sem.at[i])
        for i, (src, dst) in enumerate(
            ((ids_hbm, ids), (em_hbm, em), (be_hbm, be), (sc_hbm, sc), (v_hbm, v), (u_hbm, u))
        )
    ]
    for load in loads:
        load.start()

    barrier = pltpu.get_barrier_semaphore()
    for d in range(1, N_SEQ):
        pl.semaphore_signal(
            barrier, inc=1, device_id={"state": my_state, "seq": peer(d)},
            device_id_type=pl.DeviceIdType.MESH,
        )

    @pl.loop(1, N_STATE)
    def _(d):
        pl.semaphore_signal(
            barrier, inc=1,
            device_id={"state": lax.rem(my_state + d, N_STATE), "seq": my_seq},
            device_id_type=pl.DeviceIdType.MESH,
        )

    def block_of(k):
        return pl.ds(pl.multiple_of(k * BLOCK, BLOCK), BLOCK)

    def column(values, step):
        lane = lax.broadcasted_iota(jnp.int32, values.shape, 1)
        return jnp.sum(
            jnp.where(lane == STEPS - 1 - step, values.astype(F32), 0.0), axis=1, keepdims=True
        )

    table_rows = em.shape[0]

    def onehot(step):
        wanted = column(ids[...], step) - (my_seq * table_rows).astype(F32)
        word = lax.broadcasted_iota(jnp.int32, (SEQS, table_rows), 1).astype(F32)
        return jnp.where(word == wanted, 1.0, 0.0).astype(BF)

    def pick_send(step):
        hot = onehot(step)
        for d in list(range(1, N_SEQ)) + [0]:
            k = peer(d)
            rows = jnp.dot(hot, em[:, block_of(k)], preferred_element_type=F32).astype(BF)
            if d == 0:
                emrecv[my_seq] = rows
            else:
                emsend[k] = rows
                remote(
                    emsend.at[k], emrecv.at[my_seq], em_send, em_recv, my_state, k
                ).start()

    def pick_wait():
        wait(emrecv.at[pl.ds(0, N_SEQ - 1)], em_recv)
        wait(emsend.at[pl.ds(0, N_SEQ - 1)], em_send)

    def rows_of(c):
        return pl.ds(c * ROWS, ROWS)

    def gather_send(c, current):
        rows = rows_of(c)
        picked = jnp.sum(emrecv[:, rows, :].astype(F32), axis=0)
        wbuf[my_seq, rows, :] = (picked * current).astype(BF)
        for d in range(1, N_SEQ):
            remote(
                wbuf.at[my_seq, rows], wbuf.at[my_seq, rows], ag_send.at[c], ag_recv.at[c, my_seq],
                my_state, peer(d),
            ).start()

    loads[0].wait()
    loads[1].wait()
    loads[2].wait()
    loads[3].wait()
    pl.semaphore_wait(barrier, N_SEQ - 1 + N_STATE - 1)
    ends[my_seq] = be[:, block_of(my_seq)]
    scs[my_seq] = sc[...]
    for d in range(1, N_SEQ):
        k = peer(d)
        remote(
            be.at[:, block_of(k)], ends.at[my_seq], init_send, init_recv, my_state, k
        ).start()
        remote(scs.at[my_seq], scs.at[my_seq], cs_send.at[1], sc_recv, my_state, k).start()
    pick_send(0)

    loads[4].wait()
    sums = jnp.dot(jnp.ones((16, STATES), BF), v[...], preferred_element_type=F32)[0:1]
    csbuf[my_state] = jnp.concatenate(
        [sums[:, i * 128 : (i + 1) * 128] for i in range(4)] + [jnp.zeros((4, 128), F32)], axis=0
    )

    @pl.loop(1, N_STATE)
    def _(d):
        remote(
            csbuf.at[my_state], csbuf.at[my_state], cs_send.at[0], cs_recv,
            lax.rem(my_state + d, N_STATE), my_seq,
        ).start()

    pick_wait()
    wait(ends.at[pl.ds(0, N_SEQ - 1)], init_recv)
    wait(scs.at[pl.ds(0, N_SEQ - 1)], sc_recv)
    first = ends[...].reshape(SEQS, BLOCK)
    for c in range(CHAINS):
        gather_send(c, first[c * ROWS : (c + 1) * ROWS])

    loads[5].wait()
    wait(csbuf.at[pl.ds(0, N_STATE - 1)], cs_recv)
    mass = jnp.sum(csbuf[...], axis=0)
    mass = jnp.concatenate([mass[i : i + 1] for i in range(4)], axis=1)
    hi = mass.astype(BF).astype(F32)
    mid = (mass - hi).astype(BF).astype(F32)
    low = mass - hi - mid
    parts = jnp.concatenate([hi, mid, low, jnp.zeros((13, RANK), F32)], axis=0).astype(BF)
    for d in list(range(1, N_SEQ)) + [0]:
        k = peer(d)
        norm = lax.dot_general(
            parts, u[block_of(k), :], (((1,), (1,)), ((), ())), preferred_element_type=F32
        )[0:8]
        if d == 0:
            nrecv[my_seq] = norm
        else:
            nsend[k] = norm
            remote(nsend.at[k], nrecv.at[my_seq], n_send, n_recv, my_state, k).start()

    def first_matmul(c):
        rows = rows_of(c)
        acc = None
        for d in range(N_SEQ):
            k = peer(d)
            if d:
                wait(wbuf.at[k, rows], ag_recv.at[c, k])
            term = jnp.dot(wbuf[k, rows, :], v[block_of(k), :], preferred_element_type=F32)
            acc = term if acc is None else acc + term
        wait(wbuf.at[pl.ds(0, N_SEQ - 1), rows], ag_send.at[c])
        for i in range(HALF):
            r, l = divmod(i, 4)
            part[c * HALF + i] = acc[r * 16 : r * 16 + 16, l * 128 : l * 128 + 128].astype(BF)
        for i in range(HALF):
            tile = c * HALF + i
            owner = 2 * tile + tile % 2

            @pl.when(owner == my_state)
            def _():
                arr[my_state] = part[tile]

            @pl.when(owner != my_state)
            def _():
                remote(
                    part.at[tile], arr.at[my_state], ar_send.at[c], ar_recv, owner, my_seq
                ).start()

    chip = my_state // 2
    is_owner = lax.rem(my_state, 2) == lax.rem(chip, 2)

    def reduce_tile(c):
        @pl.when(jnp.logical_and(is_owner, chip // HALF == c))
        def _():
            wait(arr.at[pl.ds(0, N_STATE - 1)], ar_recv)
            red[...] = jnp.sum(arr[...].astype(F32), axis=0).astype(BF)
            pltpu.make_async_copy(red, msg.at[chip], msg_recv.at[c]).start()

            @pl.loop(1, N_STATE)
            def _(d):
                remote(
                    red, msg.at[chip], red_send, msg_recv.at[c],
                    lax.rem(my_state + d, N_STATE), my_seq,
                ).start()

    def second_matmul(c):
        rows = rows_of(c)
        tiles = pl.ds(c * HALF, HALF)
        wait(msg.at[tiles], msg_recv.at[c])
        m = jnp.concatenate(
            [
                jnp.concatenate([msg[c * HALF + r * 4 + l] for l in range(4)], axis=1)
                for r in range(HALF // 4)
            ],
            axis=0,
        )
        for d in list(range(1, N_SEQ)) + [0]:
            k = peer(d)
            block = lax.dot_general(
                m, u[block_of(k), :], (((1,), (1,)), ((), ())), preferred_element_type=F32
            )
            if d == 0:
                rown[rows, :] = block
            else:
                rsend[k, rows, :] = block.astype(BF)
                remote(
                    rsend.at[k, rows], rrecv.at[d - 1, rows], rs_send.at[c], rs_recv.at[c],
                    my_state, k,
                ).start()

        @pl.when(jnp.logical_and(is_owner, chip // HALF == c))
        def _():
            wait(arr.at[pl.ds(0, N_STATE - 1)], red_send)
            wait(part.at[pl.ds(0, HALF - 1)], ar_send.at[c])

        @pl.when(jnp.logical_not(jnp.logical_and(is_owner, chip // HALF == c)))
        def _():
            wait(part.at[pl.ds(0, HALF)], ar_send.at[c])

    def finish(c, step, norm):
        rows = rows_of(c)
        wait(rrecv.at[:, rows], rs_recv.at[c])
        wait(rsend.at[pl.ds(0, N_SEQ - 1), rows], rs_send.at[c])
        total = rown[rows, :] + jnp.sum(rrecv[:, rows, :].astype(F32), axis=0)
        scale = scale_column(step)[c * ROWS : (c + 1) * ROWS]
        current = total / (norm * scale)
        return current

    def scale_column(step):
        return column(scs[...].reshape(SEQS, STEPS), step)

    def step_body(step):
        for c in range(CHAINS):
            first_matmul(c)

        @pl.when(step < STEPS - 1)
        def _():
            pick_send(step + 1)

        for c in range(CHAINS):
            reduce_tile(c)
        for c in range(CHAINS):
            second_matmul(c)

        @pl.when(step == 0)
        def _():
            wait(nrecv.at[pl.ds(0, N_SEQ - 1)], n_recv)
            nrecv[0, 0:1, :] = jnp.sum(jnp.sum(nrecv[...], axis=0), axis=0, keepdims=True)

        @pl.when(step > 0)
        def _():
            wait(bk.at[pl.ds(0, SEQS - 8)], out_send)
            wait(bk.at[pl.ds(0, 8)], out_local)

        @pl.when(step < STEPS - 1)
        def _():
            pick_wait()

        norm = nrecv[0, 0:1, :]
        for c in range(CHAINS):
            current = finish(c, step, norm)
            bk[rows_of(c), :] = current

            @pl.when(step < STEPS - 1)
            def _():
                gather_send(c, current)

        for d in range(N_SEQ):
            k = peer(d)
            src = bk.at[pl.ds(pl.multiple_of(k * 8, 8), 8)]
            dst = out_hbm.at[STEPS - 1 - step, :, block_of(my_seq)]
            if d == 0:
                pltpu.make_async_copy(src, dst, out_local).start()
            else:
                remote(src, dst, out_send, out_recv, my_state, k).start()

    pl.loop(0, STEPS)(step_body)

    wait(bk.at[pl.ds(0, SEQS - 8)], out_send)
    wait(bk.at[pl.ds(0, 8)], out_local)
    wait(out_hbm.at[:, :, pl.ds(0, STATES - BLOCK)], out_recv)
    wait(ends.at[pl.ds(0, N_SEQ - 1)], init_send)
    wait(scs.at[pl.ds(0, N_SEQ - 1)], cs_send.at[1])
    wait(csbuf.at[pl.ds(0, N_STATE - 1)], cs_send.at[0])
    wait(nsend.at[pl.ds(0, N_SEQ - 1)], n_send)


def body(feature_u, feature_v, emission, word_ids, scales, backward_end):
    dma = pltpu.SemaphoreType.DMA
    scratch = [
        pltpu.VMEM(feature_u.shape, BF),
        pltpu.VMEM(feature_v.shape, BF),
        pltpu.VMEM(emission.shape, BF),
        pltpu.VMEM(word_ids.shape, jnp.int32),
        pltpu.VMEM(scales.shape, F32),
        pltpu.VMEM(backward_end.shape, F32),
        pltpu.VMEM((N_SEQ, 8, STEPS), F32),
        pltpu.VMEM((N_SEQ, 8, BLOCK), F32),
        pltpu.VMEM((N_STATE, 8, 128), F32),
        pltpu.VMEM((N_SEQ, 8, BLOCK), F32),
        pltpu.VMEM((N_SEQ, 8, BLOCK), F32),
        pltpu.VMEM((N_SEQ, SEQS, BLOCK), BF),
        pltpu.VMEM((N_SEQ, SEQS, BLOCK), BF),
        pltpu.VMEM((N_SEQ, SEQS, BLOCK), BF),
        pltpu.VMEM((TILES, 16, 128), BF),
        pltpu.VMEM((N_STATE, 16, 128), BF),
        pltpu.VMEM((16, 128), BF),
        pltpu.VMEM((TILES, 16, 128), BF),
        pltpu.VMEM((N_SEQ, SEQS, BLOCK), BF),
        pltpu.VMEM((N_SEQ - 1, SEQS, BLOCK), BF),
        pltpu.VMEM((SEQS, BLOCK), F32),
        pltpu.VMEM((SEQS, BLOCK), F32),
        dma((6,)), dma, dma, dma, dma((2,)), dma, dma, dma,
        dma, dma, dma((CHAINS,)), dma((CHAINS, N_SEQ)), dma((CHAINS,)), dma, dma, dma((CHAINS,)),
        dma((CHAINS,)), dma((CHAINS,)), dma, dma, dma,
    ]
    return pl.pallas_call(
        kernel,
        out_shape=jax.ShapeDtypeStruct((STEPS, 8, STATES), F32),
        in_specs=[pl.BlockSpec(memory_space=pl.ANY)] * 6,
        out_specs=pl.BlockSpec(memory_space=pl.ANY),
        scratch_shapes=scratch,
        compiler_params=pltpu.CompilerParams(
            collective_id=0, has_side_effects=True, vmem_limit_bytes=40 * 2**20
        ),
        name="backward_messages",
    )(feature_u, feature_v, emission, word_ids, scales, backward_end)


def solution(mesh):
    placed = (
        P("state", "seq"),
        P("state", "seq"),
        P("seq", "state"),
        P(),
        P("seq", None),
        P("seq", "state"),
    )
    return jax.shard_map(
        body, mesh=mesh, in_specs=placed, out_specs=P(None, "seq", "state"), check_vma=False
    )
```

time: 873 us -> 133 us (0.15)
  blocking collectives: 629 us -> 0 us
  waiting for transfers between devices: 194 us -> 0 us
  Pallas kernels: 0 us -> 124 us
  matrix products: 16.1 us -> 0 us
  between operations: 13.2 us -> 0.01 us
  other arithmetic: 9.88 us -> 0 us
    psum x5 -> x0, blocking collectives: 514 us -> none  [the longest x4 496 us: rank_message(): return lax.psum(partial_sum, 'state').astype(jnp.bfloat16)]
    reduce_scatter x4 -> x0, waiting for transfers between devices: 150 us -> none  [body(): lax.psum_scatter(expand(jnp.int32(0), lax.axis_size('seq') * seq_rows), '...]
    pallas_call x0 -> x1, Pallas kernels: none -> 124 us  [body(): pl.pallas_call(kernel, out_shape=jax.ShapeDtypeStruct((STEPS, 8, STATES),...]
    all_gather x4 -> x0, blocking collectives: 115 us -> none  [body(): lax.all_gather(weighted, 'seq', axis=0, tiled=True)]
    unnamed x6 -> x0, waiting for transfers between devices: 44.6 us -> none
    dot_general x9 -> x0, matrix products: 16.1 us -> none  [the longest x4 8.25 us: body(): jnp.dot(lax.all_gather(weighted, 'seq', axis=0, tiled=True), feature_v, p...]
  transfers between devices with their start and end apart: 5 -> 0, of which waited for: 5 -> 0; matrix products, arithmetic and copies ran while one was open for 0% -> 0% of each run, Pallas kernels for 0% -> 0%
where the time goes in v1:
time: 133 us
  Pallas kernels  124 us (93%)
  local copies, waits for them, and re-layouts  8.74 us (7%)
    pallas_call x1, Pallas kernels, body(): pl.pallas_call(kernel, out_shape=jax.ShapeDtypeStruct((STEPS, 8, STATES),...  124 us
    unnamed x11, local copies, waits for them, and re-layouts  8.74 us

profile of v1, /device:TPU:4, one launch (start us, length us, event | category | flops | bytes accessed | tf_op | source)
XLA Modules:
  0.0 132.9 jit_solution(15279684835625907776)
XLA Ops:
  0.0 0.8 copy.8.sc_hbm
  0.8 0.8 copy.7.ids_hbm
  1.5 0.0 copy-start
  1.5 2.5 %copy-done = bf16[1280,2048]{1,0:T(8,128)(2,1)S(1)} copy-done((bf16[1280,2048]{1,0:T(8,128)(2,1)S(1)}, bf16[1280,2048]{1,0:T(8,128)(2,1)}, u32[]{:S(2)}) %copy-start) | copy-done | bytes 5242904
  4.0 0.0 copy-start.1
  4.0 1.6 %copy-done.1 = bf16[2048,512]{1,0:T(8,128)(2,1)S(1)} copy-done((bf16[2048,512]{1,0:T(8,128)(2,1)S(1)}, bf16[2048,512]{1,0:T(8,128)(2,1)}, u32[]{:S(2)}) %copy-start.1) | copy-done | bytes 2097176
  5.6 0.0 copy-start.2
  5.6 1.6 %copy-done.2 = bf16[2048,512]{1,0:T(8,128)(2,1)S(1)} copy-done((bf16[2048,512]{1,0:T(8,128)(2,1)S(1)}, bf16[2048,512]{1,0:T(8,128)(2,1)}, u32[]{:S(2)}) %copy-start.2) | copy-done | bytes 2097176
  7.2 0.0 copy-start.3
  7.2 0.8 copy-done.3
  8.0 124.1 %backward_messages.1 = f32[4,8,2048]{2,1,0:T(8,128)S(1)} custom-call(bf16[2048,512]{1,0:T(8,128)(2,1)S(1)} %copy-done.1, bf16[2048,512]{1,0:T(8,128)(2,1)S(1)} %copy-done.2, bf16[1280,2048]{1,0:T(8,128)(2,1)S(1)} %copy-done, s32[64,4]{1,0:T(8,128)S(1)} %copy.7.ids_hbm, f32[8,4]{1,0:T(8,128)S(1)} %copy.8.sc_hbm, f32[8,2048]{1,0:T(8,128)S(1)} %copy-done.3), custom_call_target="tpu_custom_call" | custom-call | tf_op jit(solution)/shard_map/backward_messages/pallas_call | solution.py:347
  132.2 0.7 copy.10
Async XLA Ops:
  1.5 2.5 %copy-start = (bf16[1280,2048]{1,0:T(8,128)(2,1)S(1)}, bf16[1280,2048]{1,0:T(8,128)(2,1)}, u32[]{:S(2)}) copy-start(bf16[1280,2048]{1,0:T(8,128)(2,1)} %em_hbm.1) | copy-start | bytes 15728644
  4.0 1.6 %copy-start.1 = (bf16[2048,512]{1,0:T(8,128)(2,1)S(1)}, bf16[2048,512]{1,0:T(8,128)(2,1)}, u32[]{:S(2)}) copy-start(bf16[2048,512]{1,0:T(8,128)(2,1)} %u_hbm.1) | copy-start | bytes 6291460
  5.6 1.6 %copy-start.2 = (bf16[2048,512]{1,0:T(8,128)(2,1)S(1)}, bf16[2048,512]{1,0:T(8,128)(2,1)}, u32[]{:S(2)}) copy-start(bf16[2048,512]{1,0:T(8,128)(2,1)} %v_hbm.1) | copy-start | bytes 6291460
  7.2 0.8 copy-start.3

commit v2 on v0

v2 whole, which is shorter than its diff:
```python
import jax
import jax.numpy as jnp
from jax import lax
from jax.experimental import pallas as pl
from jax.experimental.pallas import tpu as pltpu
from jax.sharding import PartitionSpec as P

CHAINS = 2
STATES = 2048
RANK = 512
SEQS = 64
STEPS = 4
N_SEQ = 8
N_Z = 8
PLANE = 4
BLOCK = STATES // N_SEQ
LANES = RANK // PLANE
ROWS = SEQS // CHAINS
HOME = SEQS // N_SEQ
BF = jnp.bfloat16
F32 = jnp.float32
PLANE_TYPE = F32
SEQ_ORDER = ((2, 1), (2, 0), (1, 1), (3, 1), (1, 0), (3, 0), (0, 1))
Z_ORDER = (4, 3, 5, 2, 6, 1, 7)
PLANE_ORDER = ((1, 0), (1, 1), (0, 1))
PEERS = len(SEQ_ORDER) + len(Z_ORDER) + len(PLANE_ORDER)


def kernel(
    u_hbm, v_hbm, em_hbm, ids_hbm, sc_hbm, be_hbm, out_hbm,
    u, v, em, ids, sc, be, square, words, scale_own,
    init_out, init_in, mass_own, mass_plane, mass_z, norm_out, norm_in, norm_all,
    pick_out, pick_in, gather_in, gather_own, plane_out, plane_in, z_in, message_in,
    scatter_out, scatter_in, scatter_own, backward, last_out, last_in, last_result,
    load_sem, em_sem, init_sem, mass_sem, norm_sem, norm_all_sem, pick_sem,
    gather_send, gather_recv, plane_sem, z_sem, message_sem, scatter_sem, out_sem, out_local, last_sem,
):
    my_state = lax.axis_index("state")
    my_seq = lax.axis_index("seq")
    my_z, my_q = my_state // PLANE, lax.rem(my_state, PLANE)
    my_xh, my_core = my_q // 2, lax.rem(my_q, 2)
    my_y, my_xl = my_seq // 2, lax.rem(my_seq, 2)

    def flip(x, d):
        return 1 - x if d else x

    def seq_to(i):
        dy, dx = SEQ_ORDER[i]
        return lax.rem(my_y + dy, 4) * 2 + flip(my_xl, dx)

    def seq_from(i):
        dy, dx = SEQ_ORDER[i]
        return lax.rem(my_y + 4 - dy, 4) * 2 + flip(my_xl, dx)

    def plane_to(i):
        dx, dc = PLANE_ORDER[i]
        return flip(my_xh, dx) * 2 + flip(my_core, dc)

    def remote(src, dst, send, recv, state, seq):
        pltpu.make_async_remote_copy(
            src_ref=src, dst_ref=dst, send_sem=send, recv_sem=recv,
            device_id={"state": state, "seq": seq},
            device_id_type=pl.DeviceIdType.MESH,
        ).start()

    def to_seq(i, src, dst, sems):
        remote(src, dst, sems[0], sems[1], my_state, seq_to(i))

    def to_z(d, src, dst, sems):
        remote(src, dst, sems[0], sems[1], lax.rem(my_z + d, N_Z) * PLANE + my_q, my_seq)

    def to_plane(i, src, dst, sems):
        remote(src, dst, sems[0], sems[1], my_z * PLANE + plane_to(i), my_seq)

    def pair(ref, *index):
        return ref.at[(0,) + index], ref.at[(1,) + index]

    def wait(ref, sem):
        pltpu.make_async_copy(ref, ref, sem).wait()

    def block_of(k):
        return pl.ds(pl.multiple_of(k * BLOCK, BLOCK), BLOCK)

    def rows_of(c):
        return pl.ds(c * ROWS, ROWS)

    small = [
        pltpu.make_async_copy(src, dst, load_sem.at[i])
        for i, (src, dst) in enumerate(((ids_hbm, ids), (sc_hbm, sc), (be_hbm, be)))
    ]
    for load in small:
        load.start()
    em_loads = []
    for i in range(N_SEQ):
        k = seq_to(i) if i < N_SEQ - 1 else my_seq
        em_loads.append(
            pltpu.make_async_copy(em_hbm.at[:, block_of(k)], em.at[:, block_of(k)], em_sem.at[i])
        )
    for load in em_loads:
        load.start()
    v_load = pltpu.make_async_copy(v_hbm, v, load_sem.at[3])
    u_load = pltpu.make_async_copy(u_hbm, u, load_sem.at[4])
    v_load.start()
    u_load.start()

    barrier = pltpu.get_barrier_semaphore()

    def greet(state, seq):
        pl.semaphore_signal(
            barrier, inc=1, device_id={"state": state, "seq": seq},
            device_id_type=pl.DeviceIdType.MESH,
        )

    for d in Z_ORDER:
        greet(lax.rem(my_z + d, N_Z) * PLANE + my_q, my_seq)
    for i in range(len(SEQ_ORDER)):
        greet(my_state, seq_to(i))
    for i in range(len(PLANE_ORDER)):
        greet(my_z * PLANE + plane_to(i), my_seq)

    def columns(ref, height, width):
        square[...] = jnp.zeros_like(square)
        square[0:height, 0:width] = ref[...].astype(F32)
        return jnp.transpose(square[...])

    def column(values, step):
        lane = lax.broadcasted_iota(jnp.int32, values.shape, 1)
        return jnp.sum(jnp.where(lane == STEPS - 1 - step, values, 0.0), axis=1, keepdims=True)

    small[0].wait()
    words[...] = columns(ids, STEPS, SEQS)[0:SEQS]
    small[1].wait()
    scale_own[...] = columns(sc, STEPS, HOME)[0:HOME]
    table_rows = em.shape[0]

    def onehot(step):
        wanted = column(words[...], step) - (my_seq * table_rows).astype(F32)
        word = lax.broadcasted_iota(jnp.int32, (SEQS, table_rows), 1).astype(F32)
        return jnp.where(word == wanted, 1.0, 0.0).astype(BF)

    def pick(step, before=None):
        hot = onehot(step)
        for i in range(N_SEQ):
            k = seq_to(i) if i < N_SEQ - 1 else my_seq
            if before is not None:
                before(i)
            rows = jnp.dot(hot, em[:, block_of(k)], preferred_element_type=F32).astype(BF)
            if i == N_SEQ - 1:
                pick_in[i] = rows
            else:
                pick_out[i] = rows
                to_seq(i, pick_out.at[i], pick_in.at[i], pair(pick_sem))

    def pick_wait():
        wait(pick_in.at[pl.ds(0, N_SEQ - 1)], pick_sem.at[1])
        wait(pick_out, pick_sem.at[0])

    small[2].wait()
    for i in range(N_SEQ):
        k = seq_to(i) if i < N_SEQ - 1 else my_seq
        init_out[i, :, 0:BLOCK] = be[:, block_of(k)]
        init_out[i, :, BLOCK : BLOCK + 128] = scale_own[...]
    pl.semaphore_wait(barrier, PEERS)
    for i in range(N_SEQ - 1):
        to_seq(i, init_out.at[i], init_in.at[my_seq], pair(init_sem))
    init_in[my_seq] = init_out[N_SEQ - 1]
    pick(0, before=lambda i: em_loads[i].wait())

    v_load.wait()
    sums = jnp.dot(jnp.ones((16, STATES), BF), v[...], preferred_element_type=F32)[0:1]
    mass_own[...] = jnp.concatenate(
        [sums[:, i * 128 : (i + 1) * 128] for i in range(4)] + [jnp.zeros((4, 128), F32)], axis=0
    )
    mass_plane[3] = mass_own[...]
    for i in range(PLANE - 1):
        to_plane(i, mass_own, mass_plane.at[i], pair(mass_sem, 0))

    def send_weighted(c, current):
        rows = rows_of(c)
        picked = jnp.sum(pick_in[:, rows, :].astype(F32), axis=0)
        gather_own[rows, :] = (picked * current).astype(BF)
        for i in range(N_SEQ - 1):
            to_seq(
                i, gather_own.at[rows], gather_in.at[i, rows],
                (gather_send.at[c], gather_recv.at[c, i]),
            )

    wait(init_in.at[pl.ds(0, N_SEQ - 1)], init_sem.at[1])
    pick_wait()
    first = init_in[:, :, 0:BLOCK].reshape(SEQS, BLOCK)
    for c in range(CHAINS):
        send_weighted(c, first[c * ROWS : (c + 1) * ROWS])

    wait(mass_plane.at[pl.ds(0, 3)], mass_sem.at[1, 0])
    mass_z[my_z] = jnp.sum(mass_plane[...], axis=0)
    for d in Z_ORDER:
        to_z(d, mass_z.at[my_z], mass_z.at[my_z], pair(mass_sem, 1))

    def first_matmul(c):
        rows = rows_of(c)
        acc = jnp.dot(gather_own[rows, :], v[block_of(my_seq), :], preferred_element_type=F32)
        for i in reversed(range(N_SEQ - 1)):
            wait(gather_in.at[i, rows], gather_recv.at[c, i])
            acc += jnp.dot(
                gather_in[i, rows, :], v[block_of(seq_from(i)), :], preferred_element_type=F32
            )
        for q in range(PLANE):
            plane_out[q, rows, :] = acc[:, q * LANES : (q + 1) * LANES].astype(PLANE_TYPE)
        for i in range(PLANE - 1):
            to_plane(
                i, plane_out.at[plane_to(i), rows], plane_in.at[i, rows], pair(plane_sem, c)
            )
        wait(gather_in.at[pl.ds(0, N_SEQ - 1), rows], gather_send.at[c])

    def sum_plane(c, turn):
        rows = rows_of(c)
        wait(plane_in.at[:, rows], plane_sem.at[1, c])
        total = plane_out[my_q, rows, :].astype(F32)
        total += jnp.sum(plane_in[:, rows, :].astype(F32), axis=0)
        z_in[turn, my_z, rows, :] = total.astype(BF)
        for d in Z_ORDER:
            block = z_in.at[turn, my_z, rows]
            to_z(d, block, block, pair(z_sem, c, turn))
        wait(plane_in.at[:, rows], plane_sem.at[0, c])

    def sum_z(c, turn):
        rows = rows_of(c)
        wait(z_in.at[turn, pl.ds(0, N_Z - 1), rows], z_sem.at[1, c, turn])
        message_in[my_q, rows, :] = jnp.sum(z_in[turn, :, rows, :].astype(F32), axis=0).astype(BF)
        for i in range(PLANE - 1):
            to_plane(
                i, message_in.at[my_q, rows], message_in.at[my_q, rows], pair(message_sem, c)
            )
        wait(z_in.at[turn, pl.ds(0, N_Z - 1), rows], z_sem.at[0, c, turn])

    def message(c):
        rows = rows_of(c)
        wait(message_in.at[pl.ds(0, PLANE - 1), rows], message_sem.at[1, c])
        return jnp.concatenate([message_in[q, rows, :] for q in range(PLANE)], axis=1)

    def message_sent(c):
        wait(message_in.at[pl.ds(0, PLANE - 1), rows_of(c)], message_sem.at[0, c])

    def expand(left, k):
        return lax.dot_general(
            left, u[block_of(k), :], (((1,), (1,)), ((), ())), preferred_element_type=F32
        )

    def second_matmul(c):
        rows = rows_of(c)
        left = message(c)
        for i in range(N_SEQ - 1):
            scatter_out[i, rows, :] = expand(left, seq_to(i)).astype(BF)
            to_seq(i, scatter_out.at[i, rows], scatter_in.at[i, rows], pair(scatter_sem, c))
        scatter_own[rows, :] = expand(left, my_seq)
        message_sent(c)

    def send_outputs(step):
        for i in range(N_SEQ - 1):
            src = backward.at[pl.ds(pl.multiple_of(seq_to(i) * HOME, HOME), HOME)]
            to_seq(i, src, out_hbm.at[STEPS - 1 - step, :, block_of(my_seq)], pair(out_sem))
        pltpu.make_async_copy(
            backward.at[pl.ds(pl.multiple_of(my_seq * HOME, HOME), HOME)],
            out_hbm.at[STEPS - 1 - step, :, block_of(my_seq)],
            out_local,
        ).start()

    def outputs_sent():
        wait(backward.at[pl.ds(0, SEQS - HOME)], out_sem.at[0])
        wait(backward.at[pl.ds(0, HOME)], out_local)

    def send_norm():
        wait(mass_z.at[pl.ds(0, N_Z - 1)], mass_sem.at[1, 1])
        mass = jnp.sum(mass_z[...], axis=0)
        mass = jnp.concatenate([mass[i : i + 1] for i in range(4)], axis=1)
        hi = mass.astype(BF).astype(F32)
        mid = (mass - hi).astype(BF).astype(F32)
        low = mass - hi - mid
        parts = jnp.concatenate([hi, mid, low, jnp.zeros((13, RANK), F32)], axis=0).astype(BF)
        for i in range(N_SEQ - 1):
            norm_out[i] = expand(parts, seq_to(i))[0:8]
            to_seq(i, norm_out.at[i], norm_in.at[i], pair(norm_sem))
        norm_in[N_SEQ - 1] = expand(parts, my_seq)[0:8]

    def finish_norm():
        wait(norm_in.at[pl.ds(0, N_SEQ - 1)], norm_sem.at[1])
        total = jnp.sum(jnp.sum(norm_in[...], axis=0), axis=0, keepdims=True)
        norm_all[my_seq] = jnp.broadcast_to(total, (8, BLOCK))
        for i in range(N_SEQ - 1):
            to_seq(i, norm_all.at[my_seq], norm_all.at[my_seq], pair(norm_all_sem))

    def step_body(step):
        turn = lax.rem(step, 2)
        for c in range(CHAINS):
            first_matmul(c)
        for c in range(CHAINS):
            sum_plane(c, turn)

        @pl.when(step == 0)
        def _():
            u_load.wait()
            send_norm()

        @pl.when(step > 0)
        def _():
            send_outputs(step - 1)

        pick(step + 1)
        for c in range(CHAINS):
            sum_z(c, turn)
        for c in range(CHAINS):
            second_matmul(c)

        @pl.when(step == 0)
        def _():
            finish_norm()

        @pl.when(step > 0)
        def _():
            outputs_sent()

        pick_wait()
        norm = norm_all[my_seq][0:1]
        scales = column(init_in[:, :, BLOCK : BLOCK + 128].reshape(SEQS, 128), step)
        for c in range(CHAINS):
            rows = rows_of(c)
            wait(scatter_in.at[:, rows], scatter_sem.at[1, c])
            total = scatter_own[rows, :] + jnp.sum(scatter_in[:, rows, :].astype(F32), axis=0)
            current = total / (norm * scales[c * ROWS : (c + 1) * ROWS])
            send_weighted(c, current)
            backward[rows, :] = current
            wait(scatter_out.at[:, rows], scatter_sem.at[0, c])

    pl.loop(0, STEPS - 1)(step_body)

    for c in range(CHAINS):
        first_matmul(c)
    for c in range(CHAINS):
        sum_plane(c, (STEPS - 1) % 2)
    send_outputs(STEPS - 2)
    for c in range(CHAINS):
        sum_z(c, (STEPS - 1) % 2)
    homes = N_SEQ // CHAINS
    for c in range(CHAINS):
        left = message(c)
        for n in range(N_SEQ // 2):
            low, high = expand(left, n), expand(left, n + N_SEQ // 2)
            for h in range(homes):
                part = slice(h * HOME, (h + 1) * HOME)
                both = jnp.concatenate([low[part], high[part]], axis=0)
                last_out[c * homes + h, :, n * BLOCK : (n + 1) * BLOCK] = both.astype(BF)
        for h in range(homes):
            home = c * homes + h

            @pl.when(home != my_seq)
            def _():
                remote(
                    last_out.at[home], last_in.at[my_seq], last_sem.at[0], last_sem.at[1],
                    my_state, home,
                )

            @pl.when(home == my_seq)
            def _():
                last_in[my_seq] = last_out[home]

        message_sent(c)

    wait(norm_all.at[pl.ds(0, N_SEQ - 1)], norm_all_sem.at[1])
    scale = column(scale_own[...], STEPS - 1)
    wait(last_in.at[pl.ds(0, N_SEQ - 1)], last_sem.at[1])
    total = jnp.sum(last_in[...].astype(F32), axis=0)
    for k in range(N_SEQ):
        r, l = divmod(k, N_SEQ // 2)
        block = total[r * HOME : (r + 1) * HOME, l * BLOCK : (l + 1) * BLOCK]
        last_result[:, k * BLOCK : (k + 1) * BLOCK] = block / (norm_all[k][0:1] * scale)
    result = pltpu.make_async_copy(last_result, out_hbm.at[0], load_sem.at[0])
    result.start()

    outputs_sent()
    wait(out_hbm.at[pl.ds(1, STEPS - 1), :, pl.ds(0, STATES - BLOCK)], out_sem.at[1])
    wait(init_in.at[pl.ds(0, N_SEQ - 1)], init_sem.at[0])
    wait(mass_plane.at[pl.ds(0, 3)], mass_sem.at[0, 0])
    wait(mass_z.at[pl.ds(0, N_Z - 1)], mass_sem.at[0, 1])
    wait(norm_out, norm_sem.at[0])
    wait(norm_all.at[pl.ds(0, N_SEQ - 1)], norm_all_sem.at[0])
    wait(last_in.at[pl.ds(0, N_SEQ - 1)], last_sem.at[0])
    result.wait()


def body(feature_u, feature_v, emission, word_ids, scales, backward_end):
    dma = pltpu.SemaphoreType.DMA
    word_ids, scales = word_ids.T, scales.T
    vm = pltpu.VMEM
    scratch = [
        vm(feature_u.shape, BF),
        vm(feature_v.shape, BF),
        vm(emission.shape, BF),
        vm(word_ids.shape, jnp.int32),
        vm(scales.shape, F32),
        vm(backward_end.shape, F32),
        vm((128, 128), F32),
        vm((SEQS, 128), F32),
        vm((HOME, 128), F32),
        vm((N_SEQ, HOME, BLOCK + 128), F32),
        vm((N_SEQ, HOME, BLOCK + 128), F32),
        vm((8, 128), F32),
        vm((4, 8, 128), F32),
        vm((N_Z, 8, 128), F32),
        vm((N_SEQ - 1, 8, BLOCK), F32),
        vm((N_SEQ, 8, BLOCK), F32),
        vm((N_SEQ, 8, BLOCK), F32),
        vm((N_SEQ - 1, SEQS, BLOCK), BF),
        vm((N_SEQ, SEQS, BLOCK), BF),
        vm((N_SEQ - 1, SEQS, BLOCK), BF),
        vm((SEQS, BLOCK), BF),
        vm((PLANE, SEQS, LANES), PLANE_TYPE),
        vm((PLANE - 1, SEQS, LANES), PLANE_TYPE),
        vm((2, N_Z, SEQS, LANES), BF),
        vm((PLANE, SEQS, LANES), BF),
        vm((N_SEQ - 1, SEQS, BLOCK), BF),
        vm((N_SEQ - 1, SEQS, BLOCK), BF),
        vm((SEQS, BLOCK), F32),
        vm((SEQS, BLOCK), F32),
        vm((N_SEQ, 2 * HOME, STATES // 2), BF),
        vm((N_SEQ, 2 * HOME, STATES // 2), BF),
        vm((HOME, STATES), F32),
        dma((5,)), dma((N_SEQ,)), dma((2,)), dma((2, 2)), dma((2,)), dma((2,)), dma((2,)),
        dma((CHAINS,)), dma((CHAINS, N_SEQ - 1)), dma((2, CHAINS)), dma((2, CHAINS, 2)),
        dma((2, CHAINS)), dma((2, CHAINS)), dma((2,)), dma, dma((2,)),
    ]
    return pl.pallas_call(
        kernel,
        out_shape=jax.ShapeDtypeStruct((STEPS, HOME, STATES), F32),
        in_specs=[pl.BlockSpec(memory_space=pl.ANY)] * 6,
        out_specs=pl.BlockSpec(memory_space=pl.ANY),
        scratch_shapes=scratch,
        compiler_params=pltpu.CompilerParams(
            collective_id=0, has_side_effects=True, vmem_limit_bytes=60 * 2**20
        ),
        name="backward_messages",
    )(feature_u, feature_v, emission, word_ids, scales, backward_end)


def solution(mesh):
    placed = (
        P("state", "seq"),
        P("state", "seq"),
        P("seq", "state"),
        P(),
        P("seq", None),
        P("seq", "state"),
    )
    return jax.shard_map(
        body, mesh=mesh, in_specs=placed, out_specs=P(None, "seq", "state"), check_vma=False
    )
```

time: 873 us -> 107 us (0.12)
  blocking collectives: 629 us -> 0 us
  waiting for transfers between devices: 194 us -> 0 us
  Pallas kernels: 0 us -> 104 us
  matrix products: 16.1 us -> 0 us
  between operations: 13.2 us -> 0.01 us
  other arithmetic: 9.88 us -> 0 us
    psum x5 -> x0, blocking collectives: 514 us -> none  [the longest x4 496 us: rank_message(): return lax.psum(partial_sum, 'state').astype(jnp.bfloat16)]
    reduce_scatter x4 -> x0, waiting for transfers between devices: 150 us -> none  [body(): lax.psum_scatter(expand(jnp.int32(0), lax.axis_size('seq') * seq_rows), '...]
    all_gather x4 -> x0, blocking collectives: 115 us -> none  [body(): lax.all_gather(weighted, 'seq', axis=0, tiled=True)]
    pallas_call x0 -> x1, Pallas kernels: none -> 104 us  [body(): pl.pallas_call(kernel, out_shape=jax.ShapeDtypeStruct((STEPS, HOME, STATE...]
    unnamed x6 -> x0, waiting for transfers between devices: 44.6 us -> none
    dot_general x9 -> x0, matrix products: 16.1 us -> none  [the longest x4 8.25 us: body(): jnp.dot(lax.all_gather(weighted, 'seq', axis=0, tiled=True), feature_v, p...]
  transfers between devices with their start and end apart: 5 -> 0, of which waited for: 5 -> 0; matrix products, arithmetic and copies ran while one was open for 0% -> 0% of each run, Pallas kernels for 0% -> 0%
where the time goes in v2:
time: 107 us; the launch traced here: 106 us
  Pallas kernels  104 us (97%)
  local copies, waits for them, and re-layouts  1.67 us (2%)
    pallas_call x1, Pallas kernels, body(): pl.pallas_call(kernel, out_shape=jax.ShapeDtypeStruct((STEPS, HOME, STATE...  104 us

profile of v2, /device:TPU:4, one launch (start us, length us, event | category | flops | bytes accessed | tf_op | source)
XLA Modules:
  0.0 105.7 jit_solution(6667343483822391779)
XLA Ops:
  0.0 104.1 %backward_messages.1 = f32[4,8,2048]{2,1,0:T(8,128)} custom-call(bf16[2048,512]{1,0:T(8,128)(2,1)} %u_hbm.1, bf16[2048,512]{1,0:T(8,128)(2,1)} %v_hbm.1, bf16[1280,2048]{1,0:T(8,128)(2,1)} %em_hbm.1, s32[4,64]{1,0:T(4,128)} %bitcast.2, f32[4,8]{1,0:T(4,128)} %bitcast.3, f32[8,2048]{1,0:T(8,128)} %be_hbm.1), custom_call_target="tpu_custom_call" | custom-call | tf_op jit(solution)/shard_map/backward_messages/pallas_call | solution.py:431
  104.1 1.7 %copy.8 = f32[4,8,2048]{2,1,0:T(8,128)} copy(f32[4,8,2048]{2,1,0:T(8,128)} %backward_messages.1) | data formatting | bytes 524288
